TPU v7x, 32 devices: a whole 2x2x4 slice. The times are simulated.
32 devices in a mesh: groups: 2 (over x), ctx: 16 (over z, y, core).
Axes of the slice: x: 2, y: 2, z: 4, core: 2. Of those that a mesh axis runs over, the one named last changes fastest.
Arguments:
- context: bfloat16 [96, 256, 1024], P(('groups', 'ctx')), parts along dimension 0, may hold values from -6 to 6
- counts: int32 [32], P('groups'), parts along dimension 0, may hold values from 1 to 3, as said below
- queries: bfloat16 [128, 4096], P(('groups', 'ctx')), parts along dimension 0, may hold values from -120 to 120
- norm_gain: bfloat16 [1024], replicated, may hold values from 0.099609375 to 1.8984375
- w_query: bfloat16 [1024, 1024], replicated, may hold values from -1 to 1
- w_key: bfloat16 [1024, 1024], replicated, may hold values from -9 to 9
- w_value: bfloat16 [1024, 1024], replicated, may hold values from -0.1875 to 0.1875
- w_out: bfloat16 [1024, 1024], replicated, may hold values from -0.1875 to 0.1875
- final_gain: bfloat16 [1024], replicated, may hold values from 0.099609375 to 1.8984375
- w_kv: bfloat16 [1024, 2048], P(None, 'ctx'), may hold values from -0.1875 to 0.1875
Outputs:
- attended_context: bfloat16 [128, 4096], P(('groups', 'ctx')), parts along dimension 0
There are 2 independent parts, one for each index of `groups`. A program takes and returns all parts, laid end to end along the dimension named above; an argument that names none is the same for every part. Nothing has to cross between parts.
Inputs may be any that keep to these rules, and one draw needn't show every extreme that they name: Device d's slots are d * 3 to d * 3 + 2, and only the first counts[d] of them hold live blocks. The largest count equals 3 in every draw. For every d below 8, counts[d] + counts[d + 8] is at most 4, and equals it for some d in every draw.
All inputs are finite; a program needn't handle non-finite values.
Results may differ from a plain program's by a relative error of at most 0.025.
The roundings to bfloat16 on the way count: a program that leaves them out, or rounds other values in their place, can miss the bound.
Values may be sent and summed in bfloat16 or wider, within the bound.
No kernel may reach another device: no remote copies, remote signals or barrier semaphores. Data moves between devices by JAX's collectives and lax.ppermute only.
A program may use at most 128 MiB of HBM per device.

v0:
```python
import functools
import math

import jax
import jax.numpy as jnp
import numpy as np
from jax import lax
from jax.experimental import pallas as pl
from jax.experimental.pallas import tpu as pltpu
from jax.sharding import PartitionSpec as P

D_ENC = 1024
ENC_HEADS = 16
ENC_HD = 64
BLOCK = 256
KV_HEADS = 8
HEAD_DIM = 128
Q_HEADS = 32
GROUP = 4
QW = 4096
CAP = 3
HALF_HEADS = KV_HEADS // 2
LANES = 128
CHIPS = 8
ROWS = 4
LINES = ROWS * GROUP
F32 = jnp.float32
BF16 = jnp.bfloat16
VMEM = pl.BlockSpec(memory_space=pltpu.VMEM)
SMEM = pl.BlockSpec(memory_space=pltpu.SMEM)
HBM = pl.BlockSpec(memory_space=pltpu.HBM)
ANY = pl.BlockSpec(memory_space=pl.ANY)
PARTS = 4
PART = D_ENC // PARTS
QUERY_LINES = KV_HEADS * LINES
HALF_LOAD = (D_ENC + QUERY_LINES) // 2


def root_scale(values, gain):
    values = values.astype(F32)
    return (
        values
        * lax.rsqrt(jnp.mean(values * values, axis=-1, keepdims=True) + 1e-05)
        * gain.astype(F32)
    )


def rotary_lanes():
    position = np.arange(BLOCK, dtype=np.float64)[:, None]
    frequency = 10000.0 ** (-2.0 * np.arange(ENC_HD // 2) / ENC_HD)
    angle = position * frequency[None, :]
    cosine, sine = np.cos(angle), np.sin(angle)
    return jnp.asarray(np.stack([
        np.concatenate([cosine, cosine, cosine, cosine], axis=1),
        np.concatenate([-sine, sine, -sine, sine], axis=1),
    ]), F32)


def live_counts(counts_ref):
    me = lax.axis_index("ctx")
    own, other = counts_ref[me], counts_ref[me + 1 - 2 * lax.rem(me, 2)]
    gives = jnp.where((own == 3) & (other == 1), 1, 0)
    takes = jnp.where((own == 1) & (other == 3), 1, 0)
    return own - gives + takes, other + gives - takes, takes


def prepare_kernel(w_kv_ref, query_ref, out_ref, query_buf, sems):
    copies = [
        pltpu.make_async_copy(query_ref, query_buf, sems.at[0]),
        pltpu.make_async_copy(w_kv_ref, out_ref.at[pl.ds(0, D_ENC), :], sems.at[1]),
    ]
    for copy in copies:
        copy.start()
    copies[0].wait()
    rows = query_buf[...].astype(F32)
    for head in range(KV_HEADS):
        first = head * GROUP
        out_ref[D_ENC + head * LINES : D_ENC + (head + 1) * LINES, :] = jnp.concatenate(
            [rows[:, (first + g) * LANES : (first + g + 1) * LANES] for g in range(GROUP)], axis=0
        ).astype(BF16)
    copies[1].wait()


def prepare(w_kv, queries):
    return pl.pallas_call(
        prepare_kernel,
        out_shape=jax.ShapeDtypeStruct((D_ENC + QUERY_LINES, LANES), BF16),
        in_specs=[HBM] * 2, out_specs=VMEM,
        scratch_shapes=[pltpu.VMEM((ROWS, QW), BF16), pltpu.SemaphoreType.DMA((2,))],
        compiler_params=vmem(63),
    )(w_kv, queries)


def copy_all(pairs, sems):
    copies = [pltpu.make_async_copy(source, target, sems.at[at]) for at, (source, target) in enumerate(pairs)]
    for copy in copies:
        copy.start()
    for copy in copies:
        copy.wait()


def last_parts_kernel(*refs):
    loads, (rows_ref, upper_ref, lower_ref, across_ref, sems) = refs[:7], refs[7:]
    rows = [ref.at[pl.ds(D_ENC, QUERY_LINES), :] for ref in loads]
    copy_all([
        (loads[6].at[pl.ds(0, HALF_LOAD), :], upper_ref),
        (loads[5].at[pl.ds(HALF_LOAD, HALF_LOAD), :], lower_ref),
        (rows[5], across_ref),
    ] + [(row, rows_ref.at[at]) for at, row in enumerate(rows)], sems)


def last_parts(*loads):
    rows, upper, lower, across = pl.pallas_call(
        last_parts_kernel,
        out_shape=[
            jax.ShapeDtypeStruct((7, QUERY_LINES, LANES), BF16),
            jax.ShapeDtypeStruct((HALF_LOAD, LANES), BF16),
            jax.ShapeDtypeStruct((HALF_LOAD, LANES), BF16),
            jax.ShapeDtypeStruct((QUERY_LINES, LANES), BF16),
        ],
        in_specs=[ANY] * 7, out_specs=[ANY] * 4, scratch_shapes=[pltpu.SemaphoreType.DMA((10,))],
        compiler_params=vmem(8),
    )(*loads)
    shape = (HALF_HEADS, 2, LINES, LANES)
    return rows.reshape((7,) + shape), upper, lower, across.reshape(shape)


def project_block(x_ref, copies, table_buf, gain_ref, q_buf, k_buf, v_buf, q_ref, k_ref, v_ref):
    normed = root_scale(x_ref[...], gain_ref[...]).astype(BF16)
    for copy in copies[:2]:
        copy.wait()
    cosine, sine = table_buf[0], table_buf[1]
    lane = lax.broadcasted_iota(jnp.int32, (BLOCK, LANES), 1)
    lower = (lane % ENC_HD) < ENC_HD // 2

    def project(buf, to_ref, cosine, sine):
        for part in range(PARTS):
            values = jnp.dot(normed, buf[:, part * PART : (part + 1) * PART], preferred_element_type=F32)
            for at in range(PART // LANES):
                cut = values[:, at * LANES : (at + 1) * LANES]
                swapped = jnp.where(
                    lower, pltpu.roll(cut, LANES - ENC_HD // 2, 1), pltpu.roll(cut, ENC_HD // 2, 1))
                start = part * PART + at * LANES
                to_ref[:, start : start + LANES] = (cut * cosine + swapped * sine).astype(BF16)

    project(q_buf, q_ref, cosine * 0.125, sine * 0.125)
    for copy in copies[2:3]:
        copy.wait()
    project(k_buf, k_ref, cosine, sine)
    for copy in copies[3:4]:
        copy.wait()
    v_ref[...] = jnp.dot(normed, v_buf[...], preferred_element_type=F32).astype(BF16)


def attend_block(x_ref, copies, q_ref, k_ref, v_ref, o_buf, fgain_ref, mixed_ref, final_ref):
    first = lax.broadcasted_iota(jnp.int32, (BLOCK, LANES), 1) < ENC_HD
    for pair in range(ENC_HEADS // 2):
        cut = slice(pair * LANES, (pair + 1) * LANES)
        query, key, value = q_ref[:, cut], k_ref[:, cut], v_ref[:, cut]
        mixed = []
        for own in (first, jnp.logical_not(first)):
            scores = lax.dot_general(
                key, jnp.where(own, query, jnp.zeros_like(query)),
                (((1,), (1,)), ((), ())), preferred_element_type=F32)
            weights = jnp.exp(scores - jnp.max(scores, axis=0, keepdims=True))
            weights = (weights * (1.0 / jnp.sum(weights, axis=0, keepdims=True))).astype(BF16)
            mixed.append(lax.dot_general(
                weights, value, (((0,), (0,)), ((), ())), preferred_element_type=F32))
        mixed_ref[:, cut] = jnp.where(first, mixed[0], mixed[1]).astype(BF16)
    for copy in copies[4:]:
        copy.wait()
    residual = x_ref[...].astype(F32) + jnp.dot(mixed_ref[...], o_buf[...], preferred_element_type=F32)
    final_ref[...] = root_scale(residual, fgain_ref[...]).astype(BF16)


def first_half_kernel(context_ref, wq_ref, wk_ref, wv_ref, table_ref, gain_ref, out_ref,
                      x_ref, table_buf, q_buf, k_buf, v_buf, q_ref, k_ref, v_ref, sems):
    copies = [
        pltpu.make_async_copy(hbm, buf, sems.at[at])
        for at, (hbm, buf) in enumerate(
            ((context_ref.at[0], x_ref), (wq_ref, q_buf), (table_ref, table_buf), (wk_ref, k_buf), (wv_ref, v_buf)))
    ]
    for copy in copies:
        copy.start()
    copies[0].wait()
    project_block(x_ref, copies[1:], table_buf, gain_ref, q_buf, k_buf, v_buf, q_ref, k_ref, v_ref)
    writes = [
        pltpu.make_async_copy(buf, out_ref.at[at], sems.at[5 + at]) for at, buf in enumerate((q_ref, k_ref, v_ref))]
    for copy in writes:
        copy.start()
    for copy in writes:
        copy.wait()


def second_half_kernel(context_ref, half_ref, wo_ref, fgain_ref, out_ref,
                       x_ref, o_buf, q_ref, k_ref, v_ref, mixed_ref, final_ref, sems):
    copies = [
        pltpu.make_async_copy(hbm, buf, sems.at[at])
        for at, (hbm, buf) in enumerate(
            ((half_ref.at[0], q_ref), (half_ref.at[1], k_ref), (half_ref.at[2], v_ref), (context_ref.at[0], x_ref),
             (wo_ref, o_buf)))
    ]
    for copy in copies:
        copy.start()
    for copy in copies[:4]:
        copy.wait()
    attend_block(x_ref, copies, q_ref, k_ref, v_ref, o_buf, fgain_ref, mixed_ref, final_ref)
    copy = pltpu.make_async_copy(final_ref, out_ref.at[0], sems.at[5])
    copy.start()
    copy.wait()


def encoder_kernel(first_slot, slots, counts_ref, context_ref, taken_ref, wq_ref, wk_ref, wv_ref, wo_ref, table_ref,
                   gain_ref, fgain_ref, out_ref, mixed_ref, x_buf, q_ref, k_ref, v_ref, final_buf, table_buf,
                   q_buf, k_buf, v_buf, o_buf, sems, x_sems, out_sems):
    live, _, takes = live_counts(counts_ref)
    copies = [
        pltpu.make_async_copy(hbm, buf, sems.at[at])
        for at, (hbm, buf) in enumerate(
            ((wq_ref, q_buf), (table_ref, table_buf), (wk_ref, k_buf), (wv_ref, v_buf), (wo_ref, o_buf)))
    ]

    def read(slot):
        at = slot - first_slot
        return pltpu.make_async_copy(context_ref.at[slot], x_buf.at[at], x_sems.at[at])

    def write(slot):
        at = slot - first_slot
        return pltpu.make_async_copy(final_buf.at[at], out_ref.at[at], out_sems.at[at])

    @pl.when(live > first_slot)
    def _():
        if first_slot == 1:
            @pl.when(takes != 0)
            def _():
                pltpu.make_async_copy(taken_ref.at[CAP - 1], x_buf.at[0], x_sems.at[0]).start()

            @pl.when(takes == 0)
            def _():
                read(1).start()
        else:
            read(first_slot).start()
        for copy in copies:
            copy.start()

    for slot in slots[1:]:
        @pl.when(live > slot)
        def _():
            read(slot).start()

    for slot in slots:
        @pl.when(live > slot)
        def _():
            at = slot - first_slot
            pending = copies if slot == first_slot else []
            read(slot).wait()
            project_block(
                x_buf.at[at], pending, table_buf, gain_ref, q_buf, k_buf, v_buf, q_ref, k_ref, v_ref)
            attend_block(
                x_buf.at[at], pending, q_ref, k_ref, v_ref, o_buf, fgain_ref, mixed_ref, final_buf.at[at])
            write(slot).start()

    for slot in slots:
        @pl.when(live > slot)
        def _():
            write(slot).wait()


SQUARE, WHOLE = pltpu.VMEM((D_ENC, D_ENC), BF16), pltpu.VMEM((BLOCK, D_ENC), BF16)
TABLES = pltpu.VMEM((2, BLOCK, LANES), F32)


def vmem(mebibytes):
    return pltpu.CompilerParams(vmem_limit_bytes=mebibytes * 2**20)


def cost(flops):
    return pl.CostEstimate(flops=flops, bytes_accessed=9 * 2**20, transcendentals=2**20)


def encode(slots, counts, context, taken, weights):
    blocks = pltpu.VMEM((len(slots), BLOCK, D_ENC), BF16)
    return pl.pallas_call(
        functools.partial(encoder_kernel, slots[0], slots),
        out_shape=jax.ShapeDtypeStruct((len(slots), BLOCK, D_ENC), BF16),
        in_specs=[SMEM] + [HBM] * 7 + [VMEM] * 2,
        out_specs=HBM,
        scratch_shapes=[WHOLE, blocks, WHOLE, WHOLE, WHOLE, blocks, TABLES] + [SQUARE] * 4
        + [pltpu.SemaphoreType.DMA((5,)), pltpu.SemaphoreType.DMA((2,)), pltpu.SemaphoreType.DMA((2,))],
        compiler_params=vmem(63), cost_estimate=cost(9 * 10**9),
    )(counts, context, taken, *weights)


def first_half(context, weights):
    w_query, w_key, w_value, _, tables, gain, _ = weights
    return pl.pallas_call(
        first_half_kernel,
        out_shape=jax.ShapeDtypeStruct((3, BLOCK, D_ENC), BF16),
        in_specs=[HBM] * 5 + [VMEM],
        out_specs=HBM,
        scratch_shapes=[WHOLE, TABLES] + [SQUARE] * 3 + [WHOLE] * 3 + [pltpu.SemaphoreType.DMA((8,))],
        compiler_params=vmem(63), cost_estimate=cost(5 * 10**9),
    )(context, w_query, w_key, w_value, tables, gain)


def second_half(context, half, weights):
    return pl.pallas_call(
        second_half_kernel,
        out_shape=jax.ShapeDtypeStruct((1, BLOCK, D_ENC), BF16),
        in_specs=[HBM] * 3 + [VMEM],
        out_specs=HBM,
        scratch_shapes=[WHOLE, SQUARE] + [WHOLE] * 5 + [pltpu.SemaphoreType.DMA((6,))],
        compiler_params=vmem(63), cost_estimate=cost(5 * 10**9),
    )(context, half, weights[3], weights[6])


def three_parts(values):
    high = values.astype(BF16).astype(F32)
    middle = (values - high).astype(BF16).astype(F32)
    return high, middle, values - high - middle


def ring_chips(me):
    z, y = me // 4, lax.rem(me // 2, 2)
    place = jnp.where(z == 3, 2, jnp.where(z == 2, 3, z))
    chips = []
    for step in range(CHIPS // 2):
        at = lax.rem(place + 4 - step, 4)
        z = jnp.where(at == 2, 3, jnp.where(at == 3, 2, at))
        chips.append((2 * z + y, 2 * z + 1 - y))
    return chips


def cross_kernel(counts_ref, *refs):
    token0, token12, far0, far12 = refs[:4]
    loads, (upper_ref, lower_ref, near_ref, far_ref, across_ref) = refs[4:11], refs[11:16]
    out_ref, token_buf, weight_buf, query_buf, score_ref, value_ref, total_ref, top_ref, sum_ref = refs[16:25]
    sems, token_sems, row_sems = refs[25:]
    tokens = (token0.at[0], token12.at[0], token12.at[1], far0.at[0], far12.at[0], far12.at[1])
    me = lax.axis_index("ctx")
    core = lax.rem(me, 2)
    own_live, other_live, _ = live_counts(counts_ref)
    chips = [chip for pair in ring_chips(me) for chip in pair]
    columns = [pl.ds(pl.multiple_of(chip * LANES, LANES), LANES) for chip in chips]
    copies = [
        pltpu.make_async_copy(load.at[pl.ds(0, D_ENC), :], weight_buf.at[:, columns[at]], sems.at[at])
        for at, load in enumerate(loads)
    ]
    rest = D_ENC - HALF_LOAD
    copies.append(pltpu.make_async_copy(
        upper_ref, weight_buf.at[pl.ds(0, HALF_LOAD), columns[CHIPS - 1]], sems.at[CHIPS - 1]))
    copies.append(pltpu.make_async_copy(
        lower_ref.at[pl.ds(0, rest), :], weight_buf.at[pl.ds(HALF_LOAD, rest), columns[CHIPS - 1]], sems.at[CHIPS]))

    def fetch(at, part, source, heads):
        start = pl.multiple_of((2 * chips[at] + part) * LINES, LINES)
        copies.append(pltpu.make_async_copy(
            source, query_buf.at[heads, pl.ds(start, LINES), :], row_sems.at[len(copies) - CHIPS - 1]))

    every = slice(0, HALF_HEADS)
    for at in range(CHIPS - 1):
        fetch(at, core, near_ref.at[at, :, core], every)
        fetch(at, 1 - core, far_ref.at[at, :, core], every)
    fetch(CHIPS - 1, 1 - core, across_ref.at[:, core], every)
    for head in range(HALF_HEADS):
        start = pl.multiple_of(rest + (2 * head + core) * LINES, LINES)
        fetch(CHIPS - 1, core, lower_ref.at[pl.ds(start, LINES), :], head)

    def token_copy(at):
        return pltpu.make_async_copy(tokens[at], token_buf.at[at], token_sems.at[at])

    def live(at):
        return (own_live > at) if at < CAP else (other_live > at - CAP)

    for copy in copies:
        copy.start()
    for at in range(2 * CAP):
        @pl.when(live(at))
        def _():
            token_copy(at).start()
    total_ref[...] = jnp.zeros_like(total_ref)
    sum_ref[...] = jnp.zeros_like(sum_ref)
    top_ref[...] = jnp.full_like(top_ref, -jnp.inf)
    for copy in copies:
        copy.wait()

    for at in range(2 * CAP):
        @pl.when(live(at))
        def _():
            token_copy(at).wait()
            both = jnp.dot(token_buf[at], weight_buf[...], preferred_element_type=F32).astype(BF16)
            value_ref[at] = both[:, HALF_HEADS * LANES :]
            for head in range(HALF_HEADS):
                scores = lax.dot_general(
                    both[:, head * LANES : (head + 1) * LANES], query_buf[head],
                    (((1,), (1,)), ((), ())), preferred_element_type=F32,
                ) * (1.0 / math.sqrt(HEAD_DIM))
                score_ref[at, head] = scores
                top_ref[head] = jnp.maximum(top_ref[head], jnp.max(scores, axis=0, keepdims=True))

    for at in range(2 * CAP):
        @pl.when(live(at))
        def _():
            for head in range(HALF_HEADS):
                weights = jnp.exp(score_ref[at, head] - top_ref[head])
                sum_ref[head] += jnp.sum(weights, axis=0, keepdims=True)
                total_ref[head] += lax.dot_general(
                    weights.astype(BF16), value_ref[at, :, head * LANES : (head + 1) * LANES],
                    (((0,), (0,)), ((), ())), preferred_element_type=F32)

    lines = total_ref.shape[1]
    notes = []
    for head in range(HALF_HEADS):
        notes += list(three_parts(top_ref[head])) + list(three_parts(sum_ref[head]))
        out_ref[:, head] = total_ref[head].astype(BF16).reshape(2 * CHIPS, LINES, LANES)
    notes = jnp.concatenate(notes + [jnp.zeros((LANES - len(notes), lines), F32)], axis=0).T
    out_ref[:, HALF_HEADS] = notes.astype(BF16).reshape(2 * CHIPS, LINES, LANES)


def cross(counts, *arrays):
    lines = 2 * CHIPS * LINES
    line = pltpu.VMEM((HALF_HEADS, 1, lines), F32)
    return pl.pallas_call(
        cross_kernel,
        out_shape=jax.ShapeDtypeStruct((2 * CHIPS, HALF_HEADS + 1, LINES, LANES), BF16),
        in_specs=[SMEM] + [HBM] * 16,
        out_specs=VMEM,
        scratch_shapes=[
            pltpu.VMEM((2 * CAP, BLOCK, D_ENC), BF16),
            pltpu.VMEM((D_ENC, KV_HEADS * LANES), BF16),
            pltpu.VMEM((HALF_HEADS, lines, LANES), BF16),
            pltpu.VMEM((2 * CAP, HALF_HEADS, BLOCK, lines), F32),
            pltpu.VMEM((2 * CAP, BLOCK, HALF_HEADS * LANES), BF16),
            pltpu.VMEM((HALF_HEADS, lines, LANES), F32),
            line, line,
            pltpu.SemaphoreType.DMA((CHIPS + 1,)), pltpu.SemaphoreType.DMA((2 * CAP,)), pltpu.SemaphoreType.DMA((19,)),
        ],
        compiler_params=vmem(63),
        cost_estimate=pl.CostEstimate(flops=6 * 10**9, bytes_accessed=8 * 2**20, transcendentals=2**20),
    )(counts, *arrays)


def combine_kernel(parts_ref, out_ref):
    for core in range(2):
        pieces = [parts_ref.at[2 * chip + core] for chip in range(CHIPS)]
        notes = [piece[HALF_HEADS].astype(F32) for piece in pieces]
        for at in range(HALF_HEADS):
            lane = 6 * at
            tops = [n[:, lane : lane + 1] + n[:, lane + 1 : lane + 2] + n[:, lane + 2 : lane + 3] for n in notes]
            sums = [n[:, lane + 3 : lane + 4] + n[:, lane + 4 : lane + 5] + n[:, lane + 5 : lane + 6] for n in notes]
            top = functools.reduce(jnp.maximum, tops)
            numerator, denominator = 0.0, 0.0
            for share, amount, piece in zip([jnp.exp(t - top) for t in tops], sums, pieces):
                numerator += share * piece[at].astype(F32)
                denominator += share * amount
            lines = numerator / denominator
            for g in range(GROUP):
                start = ((2 * at + core) * GROUP + g) * LANES
                out_ref[:, start : start + LANES] = lines[g * ROWS : (g + 1) * ROWS].astype(BF16)


def combine(parts):
    return pl.pallas_call(
        combine_kernel, out_shape=jax.ShapeDtypeStruct((ROWS, QW), BF16), in_specs=[VMEM], out_specs=VMEM,
        compiler_params=vmem(8),
    )(parts)


NEXT_Z = (1, 3, 0, 2)


def exchange(values, bits):
    return lax.ppermute(values, "ctx", [(i, i ^ bits) for i in range(2 * CHIPS)])


def round_z(values, bits=0):
    return lax.ppermute(values, "ctx", [(i, (4 * NEXT_Z[i // 4] + i % 4) ^ bits) for i in range(2 * CHIPS)])


def local(context, counts, queries, norm_gain, w_query, w_key, w_value, w_out, final_gain, w_kv):
    weights = (w_query, w_key, w_value, w_out, rotary_lanes(), norm_gain, final_gain)
    load0 = prepare(w_kv, queries)
    load1, beside0, taken = round_z(load0), exchange(load0, 2), exchange(context, 1)
    half = first_half(context, weights)
    load1, beside0, taken, half = lax.optimization_barrier((load1, beside0, taken, half))
    load2, beside1 = round_z(load1), exchange(load1, 2)
    token0 = second_half(context, half, weights)
    load2, beside1, token0 = lax.optimization_barrier((load2, beside1, token0))
    load3, beside2, far0 = round_z(load2), exchange(load2, 2), exchange(token0, 1)
    token12 = encode((1, 2), counts, context, taken, weights)
    load3, beside2, far0, token12 = lax.optimization_barrier((load3, beside2, far0, token12))
    rows, upper, lower, across = last_parts(load0, beside0, load1, beside1, load2, beside2, load3)
    upper, lower, across, far_rows = exchange(upper, 2), round_z(lower), round_z(across, 1), exchange(rows, 1)
    far12 = exchange(token12, 1)
    parts = cross(
        counts, token0, token12, far0, far12, load0, beside0, load1, beside1, load2, beside2, load3,
        upper, lower, rows, far_rows, across)
    return combine(lax.all_to_all(parts, "ctx", 0, 0, tiled=True))


def rotary_tables(length, head_width):
    position = jnp.arange(length).astype(jnp.float32)[:, None]
    frequency = jnp.exp(
        jnp.arange(head_width // 2).astype(jnp.float32) * (-2.0 * math.log(10000.0) / head_width)
    )
    phase_angle = position * frequency[None, :]
    return (jnp.cos(phase_angle)[:, None, :], jnp.sin(phase_angle)[:, None, :])


def rotate(values, cosine_table, sine_table):
    half_width = values.shape[-1] // 2
    lower_half = values[..., :half_width]
    upper_half = values[..., half_width:]
    return jnp.concatenate(
        [
            lower_half * cosine_table - upper_half * sine_table,
            upper_half * cosine_table + lower_half * sine_table,
        ],
        axis=-1,
    )


def weighted_sums(cross_scores, top_scores, key_alive, cross_values):
    cross_weights = jnp.where(key_alive, jnp.exp(cross_scores - top_scores[..., None]), 0.0)
    total_rows = cross_scores.shape[0]
    denominator = jnp.sum(cross_weights, axis=-1).reshape(total_rows, Q_HEADS)
    numerator = jnp.einsum(
        "rkgt,tkd->rkgd",
        cross_weights.astype(jnp.bfloat16),
        cross_values,
        preferred_element_type=jnp.float32,
    )
    return (numerator.reshape(total_rows, QW), denominator)


def local_any(context, counts, queries, norm_gain, w_query, w_key, w_value, w_out, final_gain, w_kv):
    places = lax.axis_size("ctx")
    device_index = lax.axis_index("ctx")
    device_number = jnp.arange(places)
    own_count = jnp.sum(jnp.where(device_number == device_index, counts, 0))
    alive_slot = jnp.arange(CAP) < own_count
    slot_count = context.shape[0]
    row_count = slot_count * BLOCK
    normed = root_scale(context, norm_gain).astype(jnp.bfloat16).reshape(row_count, D_ENC)
    cosine_table, sine_table = rotary_tables(BLOCK, ENC_HD)

    def project(weight):
        return jnp.dot(normed, weight, preferred_element_type=jnp.float32).reshape(
            slot_count, BLOCK, ENC_HEADS, ENC_HD
        )

    query_rows = rotate(project(w_query), cosine_table, sine_table).astype(jnp.bfloat16)
    key_rows = rotate(project(w_key), cosine_table, sine_table).astype(jnp.bfloat16)
    value_rows = project(w_value).astype(jnp.bfloat16)
    scores = jnp.einsum(
        "sqhd,skhd->shqk", query_rows, key_rows, preferred_element_type=jnp.float32
    ) / math.sqrt(ENC_HD)
    weights = jax.nn.softmax(scores, axis=-1).astype(jnp.bfloat16)
    mixed_rows = jnp.einsum(
        "shqk,skhd->sqhd", weights, value_rows, preferred_element_type=jnp.float32
    )
    mixed_rows = mixed_rows.astype(jnp.bfloat16).reshape(row_count, D_ENC)
    residual = context.reshape(row_count, D_ENC).astype(jnp.float32) + jnp.dot(
        mixed_rows, w_out, preferred_element_type=jnp.float32
    )
    final_norm = root_scale(residual, final_gain).astype(jnp.bfloat16)
    key_value = jnp.dot(
        final_norm,
        lax.all_gather(w_kv, "ctx", axis=1, tiled=True),
        preferred_element_type=jnp.float32,
    ).astype(jnp.bfloat16)
    cross_keys = key_value[:, : KV_HEADS * HEAD_DIM].reshape(row_count, KV_HEADS, HEAD_DIM)
    cross_values = key_value[:, KV_HEADS * HEAD_DIM :].reshape(row_count, KV_HEADS, HEAD_DIM)
    every_query = lax.all_gather(queries, "ctx", axis=0, tiled=True)
    total_rows = every_query.shape[0]
    grouped = every_query.reshape(total_rows, KV_HEADS, GROUP, HEAD_DIM)
    cross_scores = jnp.einsum(
        "rkgd,tkd->rkgt", grouped, cross_keys, preferred_element_type=jnp.float32
    ) / math.sqrt(HEAD_DIM)
    key_alive = jnp.repeat(alive_slot, BLOCK)
    local_top = jnp.max(jnp.where(key_alive, cross_scores, -jnp.inf), axis=-1)
    row_top = lax.pmax(local_top.astype(jnp.bfloat16), "ctx").astype(local_top.dtype)
    numerator, denominator = weighted_sums(cross_scores, row_top, key_alive, cross_values)
    own_numerator, own_denominator = (
        lax.psum_scatter(numerator, "ctx", scatter_dimension=0, tiled=True),
        lax.psum_scatter(denominator, "ctx", scatter_dimension=0, tiled=True),
    )
    own_rows = own_numerator.shape[0]
    result = own_numerator.reshape(own_rows, Q_HEADS, HEAD_DIM) / own_denominator[..., None]
    return result.reshape(own_rows, QW).astype(jnp.bfloat16)


def solution(mesh):
    in_specs = (
        P(("groups", "ctx"), None, None),
        P("groups"),
        P(("groups", "ctx"), None),
        P(),
        P(),
        P(),
        P(),
        P(),
        P(),
        P(None, "ctx"),
    )
    out_specs = P(("groups", "ctx"), None)
    small = mesh.shape["ctx"] == 2 * CHIPS
    return jax.shard_map(local if small else local_any, mesh=mesh, in_specs=in_specs, out_specs=out_specs, check_vma=False)
```

profile of v0, /device:TPU:0, one launch (start us, length us, event | category | flops | bytes accessed | tf_op | source)
XLA Modules:
  0.0 72.4 jit_solution(1760514843998672241)
XLA Ops:
  0.0 0.5 collective-permute-start.2
  0.5 1.7 %shard_map.109.refs_0_.refs_4_ = bf16[1152,128]{1,0:T(8,128)(2,1)} custom-call(bf16[1024,128]{1,0:T(8,128)(2,1)} %w_kv_ref.1, bf16[4,4096]{1,0:T(4,128)(2,1)} %query_ref.1), custom_call_target="tpu_custom_call" | custom-call | tf_op jit(solution)/shard_map/pallas_call | solution.py:85
  2.2 2.6 %collective-permute-start.1 = (bf16[1152,128]{1,0:T(8,128)(2,1)}, bf16[1152,128]{1,0:T(8,128)(2,1)S(1)}, u32[]{:S(2)}, u32[]{:S(2)}) collective-permute-start(bf16[1152,128]{1,0:T(8,128)(2,1)} %shard_map.109.refs_0_.refs_4_), channel_id=1, source_target_pairs={{0,2},{1,3},{2,0},{3,1},{4,6},{5,7},{6,4},{7,5},{8,10},{9,11},{10,... | collective-permute-start | bytes 884744 | tf_op jit(solution)/shard_map/ppermute | solution.py:473
  4.7 1.6 %collective-permute-start = (bf16[1152,128]{1,0:T(8,128)(2,1)}, bf16[1152,128]{1,0:T(8,128)(2,1)S(1)}, u32[]{:S(2)}, u32[]{:S(2)}) collective-permute-start(bf16[1152,128]{1,0:T(8,128)(2,1)} %shard_map.109.refs_0_.refs_4_), channel_id=1, source_target_pairs={{0,4},{1,5},{2,6},{3,7},{4,12},{5,13},{6,14},{7,15},{8,0},{9,1},{1... | collective-permute-start | bytes 884744 | tf_op jit(solution)/shard_map/ppermute | solution.py:477
  6.3 6.0 %shard_map.110.half_ref = bf16[3,256,1024]{2,1,0:T(8,128)(2,1)} custom-call(bf16[3,256,1024]{2,1,0:T(8,128)(2,1)} %context_ref.5, bf16[1024,1024]{1,0:T(8,128)(2,1)} %wq_ref.3, bf16[1024,1024]{1,0:T(8,128)(2,1)} %wk_ref.3, bf16[1024,1024]{1,0:T(8,128)(2,1)} %wv_ref.3, f32[2,256,128]{2,1,0:T(8,128)} %constant.2.clone.table_ref, bf16[1024]{0:T(1024)(128)(2,1)} %gain_ref.3), custom_call_target="tpu_custom_call" | custom-call | flops 5000000000 | bytes 9437184 | tf_op jit(solution)/shard_map/pallas_call | solution.py:296
  12.6 2.4 %collective-permute-done.refs_2_.refs_6_ = bf16[1152,128]{1,0:T(8,128)(2,1)S(1)} collective-permute-done((bf16[1152,128]{1,0:T(8,128)(2,1)}, bf16[1152,128]{1,0:T(8,128)(2,1)S(1)}, u32[]{:S(2)}, u32[]{:S(2)}) %collective-permute-start) | collective-permute-done | bytes 294944 | tf_op jit(solution)/shard_map/ppermute | solution.py:477
  15.0 0.5 collective-permute-start.4
  15.5 0.9 %collective-permute-start.3 = (bf16[1152,128]{1,0:T(8,128)(2,1)S(1)}, bf16[1152,128]{1,0:T(8,128)(2,1)}, u32[]{:S(2)}, u32[]{:S(2)}) collective-permute-start(bf16[1152,128]{1,0:T(8,128)(2,1)S(1)} %collective-permute-done.refs_2_.refs_6_), channel_id=1, source_target_pairs={{0,4},{1,5},{2,6},{3,7},{4,12},{5,13},{6,14},{7,15},{8,0},{9,1},{1... | collective-permute-start | bytes 884744 | tf_op jit(solution)/shard_map/ppermute | solution.py:477
  16.4 6.0 %shard_map.111.refs_0_ = bf16[1,256,1024]{2,1,0:T(8,128)(2,1)} custom-call(bf16[3,256,1024]{2,1,0:T(8,128)(2,1)} %context_ref.5, bf16[3,256,1024]{2,1,0:T(8,128)(2,1)} %shard_map.110.half_ref, bf16[1024,1024]{1,0:T(8,128)(2,1)} %wo_ref.3, bf16[1024]{0:T(1024)(128)(2,1)} %fgain_ref.3), custom_call_target="tpu_custom_call" | custom-call | flops 5000000000 | bytes 9437184 | tf_op jit(solution)/shard_map/pallas_call | solution.py:307
  22.4 1.1 %collective-permute-done.4.refs_3_.refs_7_ = bf16[1152,128]{1,0:T(8,128)(2,1)} collective-permute-done((bf16[1152,128]{1,0:T(8,128)(2,1)S(1)}, bf16[1152,128]{1,0:T(8,128)(2,1)}, u32[]{:S(2)}, u32[]{:S(2)}) %collective-permute-start.4) | collective-permute-done | bytes 294944 | tf_op jit(solution)/shard_map/ppermute | solution.py:473
  23.5 1.4 %collective-permute-done.3.refs_4_.refs_8_ = bf16[1152,128]{1,0:T(8,128)(2,1)} collective-permute-done((bf16[1152,128]{1,0:T(8,128)(2,1)S(1)}, bf16[1152,128]{1,0:T(8,128)(2,1)}, u32[]{:S(2)}, u32[]{:S(2)}) %collective-permute-start.3) | collective-permute-done | bytes 294944 | tf_op jit(solution)/shard_map/ppermute | solution.py:477
  24.9 1.3 %collective-permute-start.6 = (bf16[1152,128]{1,0:T(8,128)(2,1)}, bf16[1152,128]{1,0:T(8,128)(2,1)}, u32[]{:S(2)}, u32[]{:S(2)}) collective-permute-start(bf16[1152,128]{1,0:T(8,128)(2,1)} %collective-permute-done.3.refs_4_.refs_8_), channel_id=1, source_target_pairs={{0,2},{1,3},{2,0},{3,1},{4,6},{5,7},{6,4},{7,5},{8,10},{9,11},{10,... | collective-permute-start | bytes 884744 | tf_op jit(solution)/shard_map/ppermute | solution.py:473
  26.1 1.2 %collective-permute-start.5 = (bf16[1152,128]{1,0:T(8,128)(2,1)}, bf16[1152,128]{1,0:T(8,128)(2,1)}, u32[]{:S(2)}, u32[]{:S(2)}) collective-permute-start(bf16[1152,128]{1,0:T(8,128)(2,1)} %collective-permute-done.3.refs_4_.refs_8_), channel_id=1, source_target_pairs={{0,4},{1,5},{2,6},{3,7},{4,12},{5,13},{6,14},{7,15},{8,0},{9,1},{1... | collective-permute-start | bytes 884744 | tf_op jit(solution)/shard_map/ppermute | solution.py:477
  27.3 9.4 %shard_map.112.refs_1_ = bf16[2,256,1024]{2,1,0:T(8,128)(2,1)} custom-call(s32[16]{0:T(128)} %counts_ref.3, bf16[3,256,1024]{2,1,0:T(8,128)(2,1)} %context_ref.5, bf16[3,256,1024]{2,1,0:T(8,128)(2,1)} %collective-permute-done.2.taken_ref, bf16[1024,1024]{1,0:T(8,128)(2,1)} %wq_ref.3, bf16[1024,1024]{1,0:T(8,128)(2,1)} %wk_ref.3, bf16[1024,1024]{1,0:T(8,128)(2,1)} %wv_ref.3, ...), custom_call_target="tpu_custom_call" | custom-call | flops 8999999488 | bytes 9437184 | tf_op jit(solution)/shard_map/pallas_call | solution.py:283
  36.9 1.1 %shard_map.113 = (bf16[7,128,128]{2,1,0:T(8,128)(2,1)S(1)}, bf16[576,128]{1,0:T(8,128)(2,1)S(1)}, bf16[576,128]{1,0:T(8,128)(2,1)S(1)}, bf16[128,128]{1,0:T(8,128)(2,1)S(1)}) custom-call(bf16[1152,128]{1,0:T(8,128)(2,1)S(1)} %copy-done, bf16[1152,128]{1,0:T(8,128)(2,1)S(1)} %collective-permute-done.1.refs_1_.refs_5_, ...), custom_call_target="tpu_custom_call" | custom-call | tf_op jit(solution)/shard_map/pallas_call | solution.py:113
  38.0 0.7 copy-done.3
  38.6 0.5 collective-permute-start.11
  39.1 3.0 %collective-permute-start.12 = (bf16[4,2,16,128]{3,2,1,0:T(8,128)(2,1)S(1)}, bf16[4,2,16,128]{3,2,1,0:T(8,128)(2,1)S(1)}, u32[]{:S(2)}, u32[]{:S(2)}) collective-permute-start(bf16[4,2,16,128]{3,2,1,0:T(8,128)(2,1)S(1)} %bitcast.4), channel_id=1, source_target_pairs={{0,5},{1,4},{2,7},{3,6},{4,13},{5,12},{6,15},{7,14},{8,1},{9,0},{1... | collective-permute-start | bytes 98312 | tf_op jit(solution)/shard_map/ppermute | solution.py:477
  42.1 3.6 %collective-permute-done.12.refs_15_ = bf16[4,2,16,128]{3,2,1,0:T(8,128)(2,1)S(1)} collective-permute-done((bf16[4,2,16,128]{3,2,1,0:T(8,128)(2,1)S(1)}, bf16[4,2,16,128]{3,2,1,0:T(8,128)(2,1)S(1)}, u32[]{:S(2)}, u32[]{:S(2)}) %collective-permute-start.12) | collective-permute-done | bytes 32800 | tf_op jit(solution)/shard_map/ppermute | solution.py:477
  45.7 0.5 collective-permute-done.10.refs_12_
  46.4 0.5 copy-done.6
  47.0 7.8 %shard_map.114 = bf16[16,5,16,128]{3,2,1,0:T(8,128)(2,1)} custom-call(s32[16]{0:T(128)} %counts_ref.3, bf16[1,256,1024]{2,1,0:T(8,128)(2,1)} %shard_map.111.refs_0_, bf16[2,256,1024]{2,1,0:T(8,128)(2,1)} %shard_map.112.refs_1_, bf16[1,256,1024]{2,1,0:T(8,128)(2,1)} %collective-permute-done.7.refs_2_, bf16[2,256,1024]{2,1,0:T(8,128)(2,1)} %collective-permute-done.8.refs_3_, ...), custom_call_target="tpu_custom_call" | custom-call | flops 6000000000 | bytes 8388608 | tf_op jit(solution)/shard_map/pallas_call | solution.py:423
  54.8 16.5 %all_to_all.5.parts_ref = bf16[16,5,16,128]{3,2,1,0:T(8,128)(2,1)S(1)} all-to-all(bf16[16,5,16,128]{3,2,1,0:T(8,128)(2,1)} %shard_map.114), channel_id=1, replica_groups=mesh['groups'=2,'ctx'=16] {'ctx'}, dimensions={0} | all-to-all | bytes 655360 | tf_op jit(solution)/shard_map/all_to_all | solution.py:498
  71.3 1.1 %shard_map.115 = bf16[4,4096]{1,0:T(4,128)(2,1)} custom-call(bf16[16,5,16,128]{3,2,1,0:T(8,128)(2,1)S(1)} %all_to_all.5.parts_ref), custom_call_target="tpu_custom_call" | custom-call | tf_op jit(solution)/shard_map/pallas_call | solution.py:463
  (26 shorter events, 0.7 us)
Async XLA Ops:
  0.0 15.0 %collective-permute-start.2 = (bf16[3,256,1024]{2,1,0:T(8,128)(2,1)}, bf16[3,256,1024]{2,1,0:T(8,128)(2,1)}, u32[]{:S(2)}, u32[]{:S(2)}) collective-permute-start(bf16[3,256,1024]{2,1,0:T(8,128)(2,1)} %context_ref.5), channel_id=1, source_target_pairs={{0,1},{1,0},{2,3},{3,2},{4,5},{5,4},{6,7},{7,6},{8,9},{9,8},{10,11... | collective-permute-start | bytes 4718600 | tf_op jit(solution)/shard_map/ppermute | solution.py:473
  2.2 10.5 %collective-permute-start.1 = (bf16[1152,128]{1,0:T(8,128)(2,1)}, bf16[1152,128]{1,0:T(8,128)(2,1)S(1)}, u32[]{:S(2)}, u32[]{:S(2)}) collective-permute-start(bf16[1152,128]{1,0:T(8,128)(2,1)} %shard_map.109.refs_0_.refs_4_), channel_id=1, source_target_pairs={{0,2},{1,3},{2,0},{3,1},{4,6},{5,7},{6,4},{7,5},{8,10},{9,11},{10,... | collective-permute-start | bytes 884744 | tf_op jit(solution)/shard_map/ppermute | solution.py:473
  4.7 10.3 %collective-permute-start = (bf16[1152,128]{1,0:T(8,128)(2,1)}, bf16[1152,128]{1,0:T(8,128)(2,1)S(1)}, u32[]{:S(2)}, u32[]{:S(2)}) collective-permute-start(bf16[1152,128]{1,0:T(8,128)(2,1)} %shard_map.109.refs_0_.refs_4_), channel_id=1, source_target_pairs={{0,4},{1,5},{2,6},{3,7},{4,12},{5,13},{6,14},{7,15},{8,0},{9,1},{1... | collective-permute-start | bytes 884744 | tf_op jit(solution)/shard_map/ppermute | solution.py:477
  12.6 24.2 %copy-start.1 = (bf16[1152,128]{1,0:T(8,128)(2,1)}, bf16[1152,128]{1,0:T(8,128)(2,1)S(1)}, u32[]{:S(2)}) copy-start(bf16[1152,128]{1,0:T(8,128)(2,1)S(1)} %collective-permute-done.1.refs_1_.refs_5_) | copy-start | bytes 884740
  15.0 21.8 %copy-start.2 = (bf16[1152,128]{1,0:T(8,128)(2,1)}, bf16[1152,128]{1,0:T(8,128)(2,1)S(1)}, u32[]{:S(2)}) copy-start(bf16[1152,128]{1,0:T(8,128)(2,1)S(1)} %collective-permute-done.refs_2_.refs_6_) | copy-start | bytes 884740
  15.0 8.4 %collective-permute-start.4 = (bf16[1152,128]{1,0:T(8,128)(2,1)S(1)}, bf16[1152,128]{1,0:T(8,128)(2,1)}, u32[]{:S(2)}, u32[]{:S(2)}) collective-permute-start(bf16[1152,128]{1,0:T(8,128)(2,1)S(1)} %collective-permute-done.refs_2_.refs_6_), channel_id=1, source_target_pairs={{0,2},{1,3},{2,0},{3,1},{4,6},{5,7},{6,4},{7,5},{8,10},{9,11},{10,... | collective-permute-start | bytes 884744 | tf_op jit(solution)/shard_map/ppermute | solution.py:473
  15.5 9.4 %collective-permute-start.3 = (bf16[1152,128]{1,0:T(8,128)(2,1)S(1)}, bf16[1152,128]{1,0:T(8,128)(2,1)}, u32[]{:S(2)}, u32[]{:S(2)}) collective-permute-start(bf16[1152,128]{1,0:T(8,128)(2,1)S(1)} %collective-permute-done.refs_2_.refs_6_), channel_id=1, source_target_pairs={{0,4},{1,5},{2,6},{3,7},{4,12},{5,13},{6,14},{7,15},{8,0},{9,1},{1... | collective-permute-start | bytes 884744 | tf_op jit(solution)/shard_map/ppermute | solution.py:477
  22.4 14.5 %copy-start = (bf16[1152,128]{1,0:T(8,128)(2,1)S(1)}, bf16[1152,128]{1,0:T(8,128)(2,1)}, u32[]{:S(2)}) copy-start(bf16[1152,128]{1,0:T(8,128)(2,1)} %shard_map.109.refs_0_.refs_4_) | copy-start | bytes 884740
  24.9 11.9 %collective-permute-start.6 = (bf16[1152,128]{1,0:T(8,128)(2,1)}, bf16[1152,128]{1,0:T(8,128)(2,1)}, u32[]{:S(2)}, u32[]{:S(2)}) collective-permute-start(bf16[1152,128]{1,0:T(8,128)(2,1)} %collective-permute-done.3.refs_4_.refs_8_), channel_id=1, source_target_pairs={{0,2},{1,3},{2,0},{3,1},{4,6},{5,7},{6,4},{7,5},{8,10},{9,11},{10,... | collective-permute-start | bytes 884744 | tf_op jit(solution)/shard_map/ppermute | solution.py:473
  26.1 10.6 %collective-permute-start.5 = (bf16[1152,128]{1,0:T(8,128)(2,1)}, bf16[1152,128]{1,0:T(8,128)(2,1)}, u32[]{:S(2)}, u32[]{:S(2)}) collective-permute-start(bf16[1152,128]{1,0:T(8,128)(2,1)} %collective-permute-done.3.refs_4_.refs_8_), channel_id=1, source_target_pairs={{0,4},{1,5},{2,6},{3,7},{4,12},{5,13},{6,14},{7,15},{8,0},{9,1},{1... | collective-permute-start | bytes 884744 | tf_op jit(solution)/shard_map/ppermute | solution.py:477
  27.3 9.5 %collective-permute-start.7 = (bf16[1,256,1024]{2,1,0:T(8,128)(2,1)}, bf16[1,256,1024]{2,1,0:T(8,128)(2,1)}, u32[]{:S(2)}, u32[]{:S(2)}) collective-permute-start(bf16[1,256,1024]{2,1,0:T(8,128)(2,1)} %shard_map.111.refs_0_), channel_id=1, source_target_pairs={{0,1},{1,0},{2,3},{3,2},{4,5},{5,4},{6,7},{7,6},{8,9},{9,8},{10,11... | collective-permute-start | bytes 1572872 | tf_op jit(solution)/shard_map/ppermute | solution.py:473
  36.8 9.5 %collective-permute-start.8 = (bf16[2,256,1024]{2,1,0:T(8,128)(2,1)}, bf16[2,256,1024]{2,1,0:T(8,128)(2,1)}, u32[]{:S(2)}, u32[]{:S(2)}) collective-permute-start(bf16[2,256,1024]{2,1,0:T(8,128)(2,1)} %shard_map.112.refs_1_), channel_id=1, source_target_pairs={{0,1},{1,0},{2,3},{3,2},{4,5},{5,4},{6,7},{7,6},{8,9},{9,8},{10,11... | collective-permute-start | bytes 3145736 | tf_op jit(solution)/shard_map/ppermute | solution.py:473
  38.0 0.7 copy-start.3
  38.6 7.6 %collective-permute-start.11 = (bf16[7,4,2,16,128]{4,3,2,1,0:T(8,128)(2,1)S(1)}, bf16[7,4,2,16,128]{4,3,2,1,0:T(8,128)(2,1)S(1)}, u32[]{:S(2)}, u32[]{:S(2)}) collective-permute-start(bf16[7,4,2,16,128]{4,3,2,1,0:T(8,128)(2,1)S(1)} %bitcast.2), channel_id=1, source_target_pairs={{0,1},{1,0},{2,3},{3,2},{4,5},{5,4},{6,7},{7,6},{8,9},{9,8},{10,11... | collective-permute-start | bytes 688136 | tf_op jit(solution)/shard_map/ppermute | solution.py:473
  39.1 6.6 %collective-permute-start.9 = (bf16[576,128]{1,0:T(8,128)(2,1)S(1)}, bf16[576,128]{1,0:T(8,128)(2,1)S(1)}, u32[]{:S(2)}, u32[]{:S(2)}) collective-permute-start(bf16[576,128]{1,0:T(8,128)(2,1)S(1)} %get-tuple-element.31), channel_id=1, source_target_pairs={{0,2},{1,3},{2,0},{3,1},{4,6},{5,7},{6,4},{7,5},{8,10},{9,11},{10,... | collective-permute-start | bytes 442376 | tf_op jit(solution)/shard_map/ppermute | solution.py:473
  39.1 7.1 %collective-permute-start.10 = (bf16[576,128]{1,0:T(8,128)(2,1)S(1)}, bf16[576,128]{1,0:T(8,128)(2,1)S(1)}, u32[]{:S(2)}, u32[]{:S(2)}) collective-permute-start(bf16[576,128]{1,0:T(8,128)(2,1)S(1)} %get-tuple-element.32), channel_id=1, source_target_pairs={{0,4},{1,5},{2,6},{3,7},{4,12},{5,13},{6,14},{7,15},{8,0},{9,1},{1... | collective-permute-start | bytes 442376 | tf_op jit(solution)/shard_map/ppermute | solution.py:477
  39.1 6.6 %collective-permute-start.12 = (bf16[4,2,16,128]{3,2,1,0:T(8,128)(2,1)S(1)}, bf16[4,2,16,128]{3,2,1,0:T(8,128)(2,1)S(1)}, u32[]{:S(2)}, u32[]{:S(2)}) collective-permute-start(bf16[4,2,16,128]{3,2,1,0:T(8,128)(2,1)S(1)} %bitcast.4), channel_id=1, source_target_pairs={{0,5},{1,4},{2,7},{3,6},{4,13},{5,12},{6,15},{7,14},{8,1},{9,0},{1... | collective-permute-start | bytes 98312 | tf_op jit(solution)/shard_map/ppermute | solution.py:477
  45.7 0.6 copy-start.7
  45.7 0.7 copy-start.5
  46.2 0.7 copy-start.6
  46.2 0.7 %copy-start.4 = (bf16[7,4,2,16,128]{4,3,2,1,0:T(8,128)(2,1)}, bf16[7,4,2,16,128]{4,3,2,1,0:T(8,128)(2,1)S(1)}, u32[]{:S(2)}) copy-start(bf16[7,4,2,16,128]{4,3,2,1,0:T(8,128)(2,1)S(1)} %collective-permute-done.11.refs_14_) | copy-start | bytes 688132
where the time goes:
time: 72.8 us; the launch traced here: 72.4 us
  Pallas kernels  33.2 us (46%)
  blocking collectives  16.5 us (23%)
  starting transfers between devices  12 us (16%)
  waiting for transfers between devices  9.23 us (13%)
  local copies, waits for them, and re-layouts  1.42 us (2%)
    all_to_all x1, blocking collectives, local(): return combine(lax.all_to_all(parts, 'ctx', 0, 0, tiled=True))  16.5 us
    pallas_call x1, Pallas kernels, encode(): pl.pallas_call(functools.partial(encoder_kernel, slots[0], slots), out_sh...  9.43 us
    ppermute x5, waiting for transfers between devices, round_z(): lax.ppermute(values, 'ctx', [(i, 4 * NEXT_Z[i // 4] + i % 4 ^ bits) for i...  7.85 us
    pallas_call x1, Pallas kernels, cross(): pl.pallas_call(cross_kernel, out_shape=jax.ShapeDtypeStruct((2 * CHIPS, H...  7.83 us
    ppermute x5, starting transfers between devices, round_z(): lax.ppermute(values, 'ctx', [(i, 4 * NEXT_Z[i // 4] + i % 4 ^ bits) for i...  6.68 us
    pallas_call x1, Pallas kernels, first_half(): pl.pallas_call(first_half_kernel, out_shape=jax.ShapeDtypeStruct((3, BLOC...  6 us
    pallas_call x1, Pallas kernels, second_half(): pl.pallas_call(second_half_kernel, out_shape=jax.ShapeDtypeStruct((1, BLO...  5.98 us
    ppermute x8, starting transfers between devices, exchange(): lax.ppermute(values, 'ctx', [(i, i ^ bits) for i in range(2 * CHIPS)])  5.31 us
  transfers between devices with their start and end apart: 13, of which 6 were waited for; matrix products, arithmetic and copies ran while one was open for 0% of the time, Pallas kernels for 33%

commit v1 on v0

--- a/solution.py
+++ b/solution.py
@@ -125,8 +125,20 @@
     return rows.reshape((7,) + shape), upper, lower, across.reshape(shape)
 
 
-def project_block(x_ref, copies, table_buf, gain_ref, q_buf, k_buf, v_buf, q_ref, k_ref, v_ref):
-    normed = root_scale(x_ref[...], gain_ref[...]).astype(BF16)
+def start_read(slot, context_ref, taken_ref, takes, x_ref, sem):
+    if slot == 1:
+        @pl.when(takes != 0)
+        def _():
+            pltpu.make_async_copy(taken_ref.at[CAP - 1], x_ref, sem).start()
+
+        @pl.when(takes == 0)
+        def _():
+            pltpu.make_async_copy(context_ref.at[slot], x_ref, sem).start()
+    else:
+        pltpu.make_async_copy(context_ref.at[slot], x_ref, sem).start()
+
+
+def project_rotated(normed, copies, table_buf, q_buf, k_buf, q_ref, k_ref):
     for copy in copies[:2]:
         copy.wait()
     cosine, sine = table_buf[0], table_buf[1]
@@ -144,12 +156,8 @@
                 to_ref[:, start : start + LANES] = (cut * cosine + swapped * sine).astype(BF16)
 
     project(q_buf, q_ref, cosine * 0.125, sine * 0.125)
-    for copy in copies[2:3]:
-        copy.wait()
+    copies[2].wait()
     project(k_buf, k_ref, cosine, sine)
-    for copy in copies[3:4]:
-        copy.wait()
-    v_ref[...] = jnp.dot(normed, v_buf[...], preferred_element_type=F32).astype(BF16)
 
 
 def attend_block(x_ref, copies, q_ref, k_ref, v_ref, o_buf, fgain_ref, mixed_ref, final_ref):
@@ -183,7 +191,10 @@
     for copy in copies:
         copy.start()
     copies[0].wait()
-    project_block(x_ref, copies[1:], table_buf, gain_ref, q_buf, k_buf, v_buf, q_ref, k_ref, v_ref)
+    normed = root_scale(x_ref[...], gain_ref[...]).astype(BF16)
+    project_rotated(normed, copies[1:4], table_buf, q_buf, k_buf, q_ref, k_ref)
+    copies[4].wait()
+    v_ref[...] = jnp.dot(normed, v_buf[...], preferred_element_type=F32).astype(BF16)
     writes = [
         pltpu.make_async_copy(buf, out_ref.at[at], sems.at[5 + at]) for at, buf in enumerate((q_ref, k_ref, v_ref))]
     for copy in writes:
@@ -192,78 +203,96 @@
         copy.wait()
 
 
-def second_half_kernel(context_ref, half_ref, wo_ref, fgain_ref, out_ref,
-                       x_ref, o_buf, q_ref, k_ref, v_ref, mixed_ref, final_ref, sems):
+def second_half_kernel(counts_ref, context_ref, taken_ref, half_ref, wo_ref, wq_ref, wk_ref, table_ref, gain_ref,
+                       fgain_ref, out_ref, next_ref, x_ref, o_buf, q_ref, k_ref, v_ref, mixed_ref, final_ref,
+                       x_next, q_buf, k_buf, table_buf, q_next, k_next, sems):
+    live, _, takes = live_counts(counts_ref)
     copies = [
         pltpu.make_async_copy(hbm, buf, sems.at[at])
         for at, (hbm, buf) in enumerate(
             ((half_ref.at[0], q_ref), (half_ref.at[1], k_ref), (half_ref.at[2], v_ref), (context_ref.at[0], x_ref),
              (wo_ref, o_buf)))
     ]
+    ahead = [
+        pltpu.make_async_copy(hbm, buf, sems.at[5 + at])
+        for at, (hbm, buf) in enumerate(((wq_ref, q_buf), (table_ref, table_buf), (wk_ref, k_buf)))
+    ]
     for copy in copies:
         copy.start()
+
+    @pl.when(live > 1)
+    def _():
+        start_read(1, context_ref, taken_ref, takes, x_next, sems.at[8])
+        for copy in ahead:
+            copy.start()
+
     for copy in copies[:4]:
         copy.wait()
     attend_block(x_ref, copies, q_ref, k_ref, v_ref, o_buf, fgain_ref, mixed_ref, final_ref)
-    copy = pltpu.make_async_copy(final_ref, out_ref.at[0], sems.at[5])
-    copy.start()
-    copy.wait()
-
-
-def encoder_kernel(first_slot, slots, counts_ref, context_ref, taken_ref, wq_ref, wk_ref, wv_ref, wo_ref, table_ref,
+    write = pltpu.make_async_copy(final_ref, out_ref.at[0], sems.at[9])
+    write.start()
+
+    @pl.when(live > 1)
+    def _():
+        pltpu.make_async_copy(context_ref.at[1], x_next, sems.at[8]).wait()
+        normed = root_scale(x_next[...], gain_ref[...]).astype(BF16)
+        project_rotated(normed, ahead, table_buf, q_buf, k_buf, q_next, k_next)
+        copy_all([(q_next, next_ref.at[0]), (k_next, next_ref.at[1])], sems)
+
+    write.wait()
+
+
+def encoder_kernel(counts_ref, context_ref, taken_ref, next_ref, wq_ref, wk_ref, wv_ref, wo_ref, table_ref,
                    gain_ref, fgain_ref, out_ref, mixed_ref, x_buf, q_ref, k_ref, v_ref, final_buf, table_buf,
                    q_buf, k_buf, v_buf, o_buf, sems, x_sems, out_sems):
     live, _, takes = live_counts(counts_ref)
+    later = [
+        pltpu.make_async_copy(hbm, buf, sems.at[at])
+        for at, (hbm, buf) in enumerate(((wq_ref, q_buf), (table_ref, table_buf), (wk_ref, k_buf)))
+    ]
     copies = [
-        pltpu.make_async_copy(hbm, buf, sems.at[at])
+        pltpu.make_async_copy(hbm, buf, sems.at[3 + at])
         for at, (hbm, buf) in enumerate(
-            ((wq_ref, q_buf), (table_ref, table_buf), (wk_ref, k_buf), (wv_ref, v_buf), (wo_ref, o_buf)))
+            ((wv_ref, v_buf), (next_ref.at[0], q_ref), (next_ref.at[1], k_ref), (wo_ref, o_buf)))
     ]
 
-    def read(slot):
-        at = slot - first_slot
-        return pltpu.make_async_copy(context_ref.at[slot], x_buf.at[at], x_sems.at[at])
-
-    def write(slot):
-        at = slot - first_slot
+    def write(at):
         return pltpu.make_async_copy(final_buf.at[at], out_ref.at[at], out_sems.at[at])
 
-    @pl.when(live > first_slot)
+    @pl.when(live > 1)
     def _():
-        if first_slot == 1:
-            @pl.when(takes != 0)
-            def _():
-                pltpu.make_async_copy(taken_ref.at[CAP - 1], x_buf.at[0], x_sems.at[0]).start()
-
-            @pl.when(takes == 0)
-            def _():
-                read(1).start()
-        else:
-            read(first_slot).start()
+        start_read(1, context_ref, taken_ref, takes, x_buf.at[0], x_sems.at[0])
         for copy in copies:
             copy.start()
 
-    for slot in slots[1:]:
-        @pl.when(live > slot)
+    @pl.when(live > 2)
+    def _():
+        start_read(2, context_ref, taken_ref, takes, x_buf.at[1], x_sems.at[1])
+        for copy in later:
+            copy.start()
+
+    for at in range(2):
+        @pl.when(live > 1 + at)
         def _():
-            read(slot).start()
-
-    for slot in slots:
-        @pl.when(live > slot)
+            pltpu.make_async_copy(context_ref.at[1 + at], x_buf.at[at], x_sems.at[at]).wait()
+            normed = root_scale(x_buf[at], gain_ref[...]).astype(BF16)
+            if at == 0:
+                copies[0].wait()
+            else:
+                project_rotated(normed, later, table_buf, q_buf, k_buf, q_ref, k_ref)
+            v_ref[...] = jnp.dot(normed, v_buf[...], preferred_element_type=F32).astype(BF16)
+            if at == 0:
+                for copy in copies[1:3]:
+                    copy.wait()
+            attend_block(
+                x_buf.at[at], [None] + copies if at == 0 else [], q_ref, k_ref, v_ref, o_buf, fgain_ref, mixed_ref,
+                final_buf.at[at])
+            write(at).start()
+
+    for at in range(2):
+        @pl.when(live > 1 + at)
         def _():
-            at = slot - first_slot
-            pending = copies if slot == first_slot else []
-            read(slot).wait()
-            project_block(
-                x_buf.at[at], pending, table_buf, gain_ref, q_buf, k_buf, v_buf, q_ref, k_ref, v_ref)
-            attend_block(
-                x_buf.at[at], pending, q_ref, k_ref, v_ref, o_buf, fgain_ref, mixed_ref, final_buf.at[at])
-            write(slot).start()
-
-    for slot in slots:
-        @pl.when(live > slot)
-        def _():
-            write(slot).wait()
+            write(at).wait()
 
 
 SQUARE, WHOLE = pltpu.VMEM((D_ENC, D_ENC), BF16), pltpu.VMEM((BLOCK, D_ENC), BF16)
@@ -278,17 +307,17 @@
     return pl.CostEstimate(flops=flops, bytes_accessed=9 * 2**20, transcendentals=2**20)
 
 
-def encode(slots, counts, context, taken, weights):
-    blocks = pltpu.VMEM((len(slots), BLOCK, D_ENC), BF16)
+def encode(counts, context, taken, ahead, weights):
+    blocks = pltpu.VMEM((2, BLOCK, D_ENC), BF16)
     return pl.pallas_call(
-        functools.partial(encoder_kernel, slots[0], slots),
-        out_shape=jax.ShapeDtypeStruct((len(slots), BLOCK, D_ENC), BF16),
-        in_specs=[SMEM] + [HBM] * 7 + [VMEM] * 2,
+        encoder_kernel,
+        out_shape=jax.ShapeDtypeStruct((2, BLOCK, D_ENC), BF16),
+        in_specs=[SMEM] + [HBM] * 8 + [VMEM] * 2,
         out_specs=HBM,
         scratch_shapes=[WHOLE, blocks, WHOLE, WHOLE, WHOLE, blocks, TABLES] + [SQUARE] * 4
-        + [pltpu.SemaphoreType.DMA((5,)), pltpu.SemaphoreType.DMA((2,)), pltpu.SemaphoreType.DMA((2,))],
+        + [pltpu.SemaphoreType.DMA((7,)), pltpu.SemaphoreType.DMA((2,)), pltpu.SemaphoreType.DMA((2,))],
         compiler_params=vmem(63), cost_estimate=cost(9 * 10**9),
-    )(counts, context, taken, *weights)
+    )(counts, context, taken, ahead, *weights)
 
 
 def first_half(context, weights):
@@ -303,15 +332,18 @@
     )(context, w_query, w_key, w_value, tables, gain)
 
 
-def second_half(context, half, weights):
+def second_half(counts, context, taken, half, weights):
+    w_query, w_key, _, w_out, tables, gain, final_gain = weights
     return pl.pallas_call(
         second_half_kernel,
-        out_shape=jax.ShapeDtypeStruct((1, BLOCK, D_ENC), BF16),
-        in_specs=[HBM] * 3 + [VMEM],
-        out_specs=HBM,
-        scratch_shapes=[WHOLE, SQUARE] + [WHOLE] * 5 + [pltpu.SemaphoreType.DMA((6,))],
-        compiler_params=vmem(63), cost_estimate=cost(5 * 10**9),
-    )(context, half, weights[3], weights[6])
+        out_shape=[
+            jax.ShapeDtypeStruct((1, BLOCK, D_ENC), BF16), jax.ShapeDtypeStruct((2, BLOCK, D_ENC), BF16)],
+        in_specs=[SMEM] + [HBM] * 7 + [VMEM] * 2,
+        out_specs=[HBM] * 2,
+        scratch_shapes=[WHOLE, SQUARE] + [WHOLE] * 6 + [SQUARE, SQUARE, TABLES, WHOLE, WHOLE]
+        + [pltpu.SemaphoreType.DMA((10,))],
+        compiler_params=vmem(63), cost_estimate=cost(6 * 10**9),
+    )(counts, context, taken, half, w_out, w_query, w_key, tables, gain, final_gain)
 
 
 def three_parts(values):
@@ -484,10 +516,10 @@
     half = first_half(context, weights)
     load1, beside0, taken, half = lax.optimization_barrier((load1, beside0, taken, half))
     load2, beside1 = round_z(load1), exchange(load1, 2)
-    token0 = second_half(context, half, weights)
-    load2, beside1, token0 = lax.optimization_barrier((load2, beside1, token0))
+    token0, ahead = second_half(counts, context, taken, half, weights)
+    load2, beside1, token0, ahead = lax.optimization_barrier((load2, beside1, token0, ahead))
     load3, beside2, far0 = round_z(load2), exchange(load2, 2), exchange(token0, 1)
-    token12 = encode((1, 2), counts, context, taken, weights)
+    token12 = encode(counts, context, taken, ahead, weights)
     load3, beside2, far0, token12 = lax.optimization_barrier((load3, beside2, far0, token12))
     rows, upper, lower, across = last_parts(load0, beside0, load1, beside1, load2, beside2, load3)
     upper, lower, across, far_rows = exchange(upper, 2), round_z(lower), round_z(across, 1), exchange(rows, 1)

time: 72.8 us -> 79 us (1.085)
  starting transfers between devices: 12 us -> 17.7 us
  waiting for transfers between devices: 9.23 us -> 6.95 us
  local copies, waits for them, and re-layouts: 1.42 us -> 3.11 us
    ppermute x5, starting transfers between devices: 6.68 us -> 12.8 us  [round_z(): lax.ppermute(values, 'ctx', [(i, 4 * NEXT_Z[i // 4] + i % 4 ^ bits) for i...]
    unnamed x16 -> x20, local copies, waits for them, and re-layouts: 1.42 us -> 3.11 us
    ppermute x5, waiting for transfers between devices: 7.85 us -> 6.63 us  [round_z(): lax.ppermute(values, 'ctx', [(i, 4 * NEXT_Z[i // 4] + i % 4 ^ bits) for i...]
    ppermute x8, waiting for transfers between devices: 1.38 us -> 0.32 us  [exchange(): lax.ppermute(values, 'ctx', [(i, i ^ bits) for i in range(2 * CHIPS)])]
  transfers between devices with their start and end apart: 13 -> 13, of which waited for: 6 -> 3; matrix products, arithmetic and copies ran while one was open for 0% -> 0% of each run, Pallas kernels for 33% -> 32%
where the time goes in v1:
time: 79 us; the launch traced here: 78.2 us
  Pallas kernels  33.8 us (43%)
  starting transfers between devices  17.7 us (22%)
  blocking collectives  16.4 us (21%)
  waiting for transfers between devices  6.95 us (9%)
  local copies, waits for them, and re-layouts  3.11 us (4%)
    all_to_all x1, blocking collectives, local(): return combine(lax.all_to_all(parts, 'ctx', 0, 0, tiled=True))  16.4 us
    ppermute x5, starting transfers between devices, round_z(): lax.ppermute(values, 'ctx', [(i, 4 * NEXT_Z[i // 4] + i % 4 ^ bits) for i...  12.8 us
    pallas_call x1, Pallas kernels, second_half(): pl.pallas_call(second_half_kernel, out_shape=[jax.ShapeDtypeStruct((1, BL...  8.24 us
    pallas_call x1, Pallas kernels, cross(): pl.pallas_call(cross_kernel, out_shape=jax.ShapeDtypeStruct((2 * CHIPS, H...  7.84 us
    pallas_call x1, Pallas kernels, encode(): pl.pallas_call(encoder_kernel, out_shape=jax.ShapeDtypeStruct((2, BLOCK,...  7.83 us
    ppermute x5, waiting for transfers between devices, round_z(): lax.ppermute(values, 'ctx', [(i, 4 * NEXT_Z[i // 4] + i % 4 ^ bits) for i...  6.63 us
    pallas_call x1, Pallas kernels, first_half(): pl.pallas_call(first_half_kernel, out_shape=jax.ShapeDtypeStruct((3, BLOC...  6 us
    ppermute x8, starting transfers between devices, exchange(): lax.ppermute(values, 'ctx', [(i, i ^ bits) for i in range(2 * CHIPS)])  4.87 us
  transfers between devices with their start and end apart: 13, of which 3 were waited for; matrix products, arithmetic and copies ran while one was open for 0% of the time, Pallas kernels for 32%

profile of v1, /device:TPU:0, one launch (start us, length us, event | category | flops | bytes accessed | tf_op | source)
XLA Modules:
  0.0 78.2 jit_solution(6634360729977109509)
XLA Ops:
  0.0 0.5 collective-permute-start.2
  0.5 1.7 %shard_map.109.refs_0_.refs_4_ = bf16[1152,128]{1,0:T(8,128)(2,1)} custom-call(bf16[1024,128]{1,0:T(8,128)(2,1)} %w_kv_ref.1, bf16[4,4096]{1,0:T(4,128)(2,1)} %query_ref.1), custom_call_target="tpu_custom_call" | custom-call | tf_op jit(solution)/shard_map/pallas_call | solution.py:85
  2.2 2.6 %collective-permute-start.1 = (bf16[1152,128]{1,0:T(8,128)(2,1)}, bf16[1152,128]{1,0:T(8,128)(2,1)S(1)}, u32[]{:S(2)}, u32[]{:S(2)}) collective-permute-start(bf16[1152,128]{1,0:T(8,128)(2,1)} %shard_map.109.refs_0_.refs_4_), channel_id=1, source_target_pairs={{0,2},{1,3},{2,0},{3,1},{4,6},{5,7},{6,4},{7,5},{8,10},{9,11},{10,... | collective-permute-start | bytes 884744 | tf_op jit(solution)/shard_map/ppermute | solution.py:505
  4.7 1.6 %collective-permute-start = (bf16[1152,128]{1,0:T(8,128)(2,1)}, bf16[1152,128]{1,0:T(8,128)(2,1)S(1)}, u32[]{:S(2)}, u32[]{:S(2)}) collective-permute-start(bf16[1152,128]{1,0:T(8,128)(2,1)} %shard_map.109.refs_0_.refs_4_), channel_id=1, source_target_pairs={{0,4},{1,5},{2,6},{3,7},{4,12},{5,13},{6,14},{7,15},{8,0},{9,1},{1... | collective-permute-start | bytes 884744 | tf_op jit(solution)/shard_map/ppermute | solution.py:509
  6.3 6.0 %shard_map.110.half_ref = bf16[3,256,1024]{2,1,0:T(8,128)(2,1)} custom-call(bf16[3,256,1024]{2,1,0:T(8,128)(2,1)} %context_ref.5, bf16[1024,1024]{1,0:T(8,128)(2,1)} %wq_ref.5, bf16[1024,1024]{1,0:T(8,128)(2,1)} %wk_ref.5, bf16[1024,1024]{1,0:T(8,128)(2,1)} %wv_ref.3, f32[2,256,128]{2,1,0:T(8,128)} %constant.2.clone.table_ref, bf16[1024]{0:T(1024)(128)(2,1)} %gain_ref.5), custom_call_target="tpu_custom_call" | custom-call | flops 5000000000 | bytes 9437184 | tf_op jit(solution)/shard_map/pallas_call | solution.py:325
  12.3 0.3 collective-permute-done.1.refs_1_.refs_5_
  12.6 2.4 %collective-permute-done.refs_2_.refs_6_ = bf16[1152,128]{1,0:T(8,128)(2,1)S(1)} collective-permute-done((bf16[1152,128]{1,0:T(8,128)(2,1)}, bf16[1152,128]{1,0:T(8,128)(2,1)S(1)}, u32[]{:S(2)}, u32[]{:S(2)}) %collective-permute-start) | collective-permute-done | bytes 294944 | tf_op jit(solution)/shard_map/ppermute | solution.py:509
  15.0 0.5 collective-permute-start.4
  15.5 0.9 %collective-permute-start.3 = (bf16[1152,128]{1,0:T(8,128)(2,1)S(1)}, bf16[1152,128]{1,0:T(8,128)(2,1)}, u32[]{:S(2)}, u32[]{:S(2)}) collective-permute-start(bf16[1152,128]{1,0:T(8,128)(2,1)S(1)} %collective-permute-done.refs_2_.refs_6_), channel_id=1, source_target_pairs={{0,4},{1,5},{2,6},{3,7},{4,12},{5,13},{6,14},{7,15},{8,0},{9,1},{1... | collective-permute-start | bytes 884744 | tf_op jit(solution)/shard_map/ppermute | solution.py:509
  16.4 8.2 %shard_map.111 = (bf16[1,256,1024]{2,1,0:T(8,128)(2,1)}, bf16[2,256,1024]{2,1,0:T(8,128)(2,1)}) custom-call(s32[16]{0:T(128)} %counts_ref.5, bf16[3,256,1024]{2,1,0:T(8,128)(2,1)} %context_ref.5, bf16[3,256,1024]{2,1,0:T(8,128)(2,1)} %collective-permute-done.2.taken_ref, bf16[3,256,1024]{2,1,0:T(8,128)(2,1)} %shard_map.110.half_ref, ...), custom_call_target="tpu_custom_call" | custom-call | flops 6000000000 | bytes 9437184 | tf_op jit(solution)/shard_map/pallas_call | solution.py:337
  24.7 0.7 copy-done.3
  25.4 0.7 collective-permute-start.6
  26.1 4.1 %collective-permute-start.5 = (bf16[1152,128]{1,0:T(8,128)(2,1)}, bf16[1152,128]{1,0:T(8,128)(2,1)}, u32[]{:S(2)}, u32[]{:S(2)}) collective-permute-start(bf16[1152,128]{1,0:T(8,128)(2,1)} %collective-permute-done.3.refs_4_.refs_8_), channel_id=1, source_target_pairs={{0,4},{1,5},{2,6},{3,7},{4,12},{5,13},{6,14},{7,15},{8,0},{9,1},{1... | collective-permute-start | bytes 884744 | tf_op jit(solution)/shard_map/ppermute | solution.py:509
  30.2 7.8 %shard_map.112.refs_1_ = bf16[2,256,1024]{2,1,0:T(8,128)(2,1)} custom-call(s32[16]{0:T(128)} %counts_ref.5, bf16[3,256,1024]{2,1,0:T(8,128)(2,1)} %context_ref.5, bf16[3,256,1024]{2,1,0:T(8,128)(2,1)} %collective-permute-done.2.taken_ref, bf16[2,256,1024]{2,1,0:T(8,128)(2,1)} %get-tuple-element.30.next_ref, bf16[1024,1024]{1,0:T(8,128)(2,1)} %wq_ref.5, ...), custom_call_target="tpu_custom_call" | custom-call | flops 8999999488 | bytes 9437184 | tf_op jit(solution)/shard_map/pallas_call | solution.py:312
  38.2 1.0 %copy-done.4 = bf16[1152,128]{1,0:T(8,128)(2,1)S(1)} copy-done((bf16[1152,128]{1,0:T(8,128)(2,1)S(1)}, bf16[1152,128]{1,0:T(8,128)(2,1)}, u32[]{:S(2)}) %copy-start.4) | copy-done | bytes 294936
  39.1 1.1 %shard_map.113 = (bf16[7,128,128]{2,1,0:T(8,128)(2,1)S(1)}, bf16[576,128]{1,0:T(8,128)(2,1)S(1)}, bf16[576,128]{1,0:T(8,128)(2,1)S(1)}, bf16[128,128]{1,0:T(8,128)(2,1)S(1)}) custom-call(bf16[1152,128]{1,0:T(8,128)(2,1)S(1)} %copy-done, bf16[1152,128]{1,0:T(8,128)(2,1)S(1)} %collective-permute-done.1.refs_1_.refs_5_, ...), custom_call_target="tpu_custom_call" | custom-call | tf_op jit(solution)/shard_map/pallas_call | solution.py:113
  40.2 0.7 copy-done.5
  40.9 0.5 collective-permute-start.11
  41.5 6.3 %collective-permute-start.10 = (bf16[576,128]{1,0:T(8,128)(2,1)S(1)}, bf16[576,128]{1,0:T(8,128)(2,1)S(1)}, u32[]{:S(2)}, u32[]{:S(2)}) collective-permute-start(bf16[576,128]{1,0:T(8,128)(2,1)S(1)} %get-tuple-element.38), channel_id=1, source_target_pairs={{0,4},{1,5},{2,6},{3,7},{4,12},{5,13},{6,14},{7,15},{8,0},{9,1},{1... | collective-permute-start | bytes 442376 | tf_op jit(solution)/shard_map/ppermute | solution.py:509
  47.7 4.2 %collective-permute-done.12.refs_15_ = bf16[4,2,16,128]{3,2,1,0:T(8,128)(2,1)S(1)} collective-permute-done((bf16[4,2,16,128]{3,2,1,0:T(8,128)(2,1)S(1)}, bf16[4,2,16,128]{3,2,1,0:T(8,128)(2,1)S(1)}, u32[]{:S(2)}, u32[]{:S(2)}) %collective-permute-start.12) | collective-permute-done | bytes 32800 | tf_op jit(solution)/shard_map/ppermute | solution.py:509
  52.0 0.6 copy-done.9
  52.8 7.8 %shard_map.114 = bf16[16,5,16,128]{3,2,1,0:T(8,128)(2,1)} custom-call(s32[16]{0:T(128)} %counts_ref.5, bf16[1,256,1024]{2,1,0:T(8,128)(2,1)} %get-tuple-element.28.refs_0_, bf16[2,256,1024]{2,1,0:T(8,128)(2,1)} %shard_map.112.refs_1_, bf16[1,256,1024]{2,1,0:T(8,128)(2,1)} %collective-permute-done.7.refs_2_, ...), custom_call_target="tpu_custom_call" | custom-call | flops 6000000000 | bytes 8388608 | tf_op jit(solution)/shard_map/pallas_call | solution.py:455
  60.6 16.4 %all_to_all.5.parts_ref = bf16[16,5,16,128]{3,2,1,0:T(8,128)(2,1)S(1)} all-to-all(bf16[16,5,16,128]{3,2,1,0:T(8,128)(2,1)} %shard_map.114), channel_id=1, replica_groups=mesh['groups'=2,'ctx'=16] {'ctx'}, dimensions={0} | all-to-all | bytes 655360 | tf_op jit(solution)/shard_map/all_to_all | solution.py:530
  77.1 1.1 %shard_map.115 = bf16[4,4096]{1,0:T(4,128)(2,1)} custom-call(bf16[16,5,16,128]{3,2,1,0:T(8,128)(2,1)S(1)} %all_to_all.5.parts_ref), custom_call_target="tpu_custom_call" | custom-call | tf_op jit(solution)/shard_map/pallas_call | solution.py:495
  (30 shorter events, 0.4 us)
Async XLA Ops:
  0.0 15.0 %collective-permute-start.2 = (bf16[3,256,1024]{2,1,0:T(8,128)(2,1)}, bf16[3,256,1024]{2,1,0:T(8,128)(2,1)}, u32[]{:S(2)}, u32[]{:S(2)}) collective-permute-start(bf16[3,256,1024]{2,1,0:T(8,128)(2,1)} %context_ref.5), channel_id=1, source_target_pairs={{0,1},{1,0},{2,3},{3,2},{4,5},{5,4},{6,7},{7,6},{8,9},{9,8},{10,11... | collective-permute-start | bytes 4718600 | tf_op jit(solution)/shard_map/ppermute | solution.py:505
  2.2 10.5 %collective-permute-start.1 = (bf16[1152,128]{1,0:T(8,128)(2,1)}, bf16[1152,128]{1,0:T(8,128)(2,1)S(1)}, u32[]{:S(2)}, u32[]{:S(2)}) collective-permute-start(bf16[1152,128]{1,0:T(8,128)(2,1)} %shard_map.109.refs_0_.refs_4_), channel_id=1, source_target_pairs={{0,2},{1,3},{2,0},{3,1},{4,6},{5,7},{6,4},{7,5},{8,10},{9,11},{10,... | collective-permute-start | bytes 884744 | tf_op jit(solution)/shard_map/ppermute | solution.py:505
  4.7 10.3 %collective-permute-start = (bf16[1152,128]{1,0:T(8,128)(2,1)}, bf16[1152,128]{1,0:T(8,128)(2,1)S(1)}, u32[]{:S(2)}, u32[]{:S(2)}) collective-permute-start(bf16[1152,128]{1,0:T(8,128)(2,1)} %shard_map.109.refs_0_.refs_4_), channel_id=1, source_target_pairs={{0,4},{1,5},{2,6},{3,7},{4,12},{5,13},{6,14},{7,15},{8,0},{9,1},{1... | collective-permute-start | bytes 884744 | tf_op jit(solution)/shard_map/ppermute | solution.py:509
  12.6 25.5 %copy-start.1 = (bf16[1152,128]{1,0:T(8,128)(2,1)}, bf16[1152,128]{1,0:T(8,128)(2,1)S(1)}, u32[]{:S(2)}) copy-start(bf16[1152,128]{1,0:T(8,128)(2,1)S(1)} %collective-permute-done.1.refs_1_.refs_5_) | copy-start | bytes 884740
  15.0 23.1 %copy-start.2 = (bf16[1152,128]{1,0:T(8,128)(2,1)}, bf16[1152,128]{1,0:T(8,128)(2,1)S(1)}, u32[]{:S(2)}) copy-start(bf16[1152,128]{1,0:T(8,128)(2,1)S(1)} %collective-permute-done.refs_2_.refs_6_) | copy-start | bytes 884740
  15.0 9.6 %collective-permute-start.4 = (bf16[1152,128]{1,0:T(8,128)(2,1)S(1)}, bf16[1152,128]{1,0:T(8,128)(2,1)S(1)}, u32[]{:S(2)}, u32[]{:S(2)}) collective-permute-start(bf16[1152,128]{1,0:T(8,128)(2,1)S(1)} %collective-permute-done.refs_2_.refs_6_), channel_id=1, source_target_pairs={{0,2},{1,3},{2,0},{3,1},{4,6},{5,7},{6,4},{7,5},{8,10},{9,11},{10,... | collective-permute-start | bytes 884744 | tf_op jit(solution)/shard_map/ppermute | solution.py:505
  15.5 9.9 %collective-permute-start.3 = (bf16[1152,128]{1,0:T(8,128)(2,1)S(1)}, bf16[1152,128]{1,0:T(8,128)(2,1)}, u32[]{:S(2)}, u32[]{:S(2)}) collective-permute-start(bf16[1152,128]{1,0:T(8,128)(2,1)S(1)} %collective-permute-done.refs_2_.refs_6_), channel_id=1, source_target_pairs={{0,4},{1,5},{2,6},{3,7},{4,12},{5,13},{6,14},{7,15},{8,0},{9,1},{1... | collective-permute-start | bytes 884744 | tf_op jit(solution)/shard_map/ppermute | solution.py:509
  24.7 0.7 copy-start.3
  25.4 12.8 %copy-start = (bf16[1152,128]{1,0:T(8,128)(2,1)S(1)}, bf16[1152,128]{1,0:T(8,128)(2,1)}, u32[]{:S(2)}) copy-start(bf16[1152,128]{1,0:T(8,128)(2,1)} %shard_map.109.refs_0_.refs_4_) | copy-start | bytes 884740
  25.4 12.6 %collective-permute-start.6 = (bf16[1152,128]{1,0:T(8,128)(2,1)}, bf16[1152,128]{1,0:T(8,128)(2,1)}, u32[]{:S(2)}, u32[]{:S(2)}) collective-permute-start(bf16[1152,128]{1,0:T(8,128)(2,1)} %collective-permute-done.3.refs_4_.refs_8_), channel_id=1, source_target_pairs={{0,2},{1,3},{2,0},{3,1},{4,6},{5,7},{6,4},{7,5},{8,10},{9,11},{10,... | collective-permute-start | bytes 884744 | tf_op jit(solution)/shard_map/ppermute | solution.py:505
  26.1 11.9 %collective-permute-start.5 = (bf16[1152,128]{1,0:T(8,128)(2,1)}, bf16[1152,128]{1,0:T(8,128)(2,1)}, u32[]{:S(2)}, u32[]{:S(2)}) collective-permute-start(bf16[1152,128]{1,0:T(8,128)(2,1)} %collective-permute-done.3.refs_4_.refs_8_), channel_id=1, source_target_pairs={{0,4},{1,5},{2,6},{3,7},{4,12},{5,13},{6,14},{7,15},{8,0},{9,1},{1... | collective-permute-start | bytes 884744 | tf_op jit(solution)/shard_map/ppermute | solution.py:509
  30.2 7.9 %collective-permute-start.7 = (bf16[1,256,1024]{2,1,0:T(8,128)(2,1)}, bf16[1,256,1024]{2,1,0:T(8,128)(2,1)}, u32[]{:S(2)}, u32[]{:S(2)}) collective-permute-start(bf16[1,256,1024]{2,1,0:T(8,128)(2,1)} %get-tuple-element.28.refs_0_), channel_id=1, source_target_pairs={{0,1},{1,0},{2,3},{3,2},{4,5},{5,4},{6,7},{7,6},{8,9},{9,8},{10,11... | collective-permute-start | bytes 1572872 | tf_op jit(solution)/shard_map/ppermute | solution.py:505
  38.0 14.0 %collective-permute-start.8 = (bf16[2,256,1024]{2,1,0:T(8,128)(2,1)}, bf16[2,256,1024]{2,1,0:T(8,128)(2,1)}, u32[]{:S(2)}, u32[]{:S(2)}) collective-permute-start(bf16[2,256,1024]{2,1,0:T(8,128)(2,1)} %shard_map.112.refs_1_), channel_id=1, source_target_pairs={{0,1},{1,0},{2,3},{3,2},{4,5},{5,4},{6,7},{7,6},{8,9},{9,8},{10,11... | collective-permute-start | bytes 3145736 | tf_op jit(solution)/shard_map/ppermute | solution.py:505
  38.2 1.0 %copy-start.4 = (bf16[1152,128]{1,0:T(8,128)(2,1)S(1)}, bf16[1152,128]{1,0:T(8,128)(2,1)}, u32[]{:S(2)}) copy-start(bf16[1152,128]{1,0:T(8,128)(2,1)} %copy-done.3) | copy-start | bytes 884740
  40.2 0.7 copy-start.5
  40.9 11.1 %collective-permute-start.11 = (bf16[7,4,2,16,128]{4,3,2,1,0:T(8,128)(2,1)S(1)}, bf16[7,4,2,16,128]{4,3,2,1,0:T(8,128)(2,1)S(1)}, u32[]{:S(2)}, u32[]{:S(2)}) collective-permute-start(bf16[7,4,2,16,128]{4,3,2,1,0:T(8,128)(2,1)S(1)} %bitcast.2), channel_id=1, source_target_pairs={{0,1},{1,0},{2,3},{3,2},{4,5},{5,4},{6,7},{7,6},{8,9},{9,8},{10,11... | collective-permute-start | bytes 688136 | tf_op jit(solution)/shard_map/ppermute | solution.py:505
  41.4 10.6 %collective-permute-start.9 = (bf16[576,128]{1,0:T(8,128)(2,1)S(1)}, bf16[576,128]{1,0:T(8,128)(2,1)S(1)}, u32[]{:S(2)}, u32[]{:S(2)}) collective-permute-start(bf16[576,128]{1,0:T(8,128)(2,1)S(1)} %get-tuple-element.37), channel_id=1, source_target_pairs={{0,2},{1,3},{2,0},{3,1},{4,6},{5,7},{6,4},{7,5},{8,10},{9,11},{10,... | collective-permute-start | bytes 442376 | tf_op jit(solution)/shard_map/ppermute | solution.py:505
  41.5 10.5 %collective-permute-start.10 = (bf16[576,128]{1,0:T(8,128)(2,1)S(1)}, bf16[576,128]{1,0:T(8,128)(2,1)S(1)}, u32[]{:S(2)}, u32[]{:S(2)}) collective-permute-start(bf16[576,128]{1,0:T(8,128)(2,1)S(1)} %get-tuple-element.38), channel_id=1, source_target_pairs={{0,4},{1,5},{2,6},{3,7},{4,12},{5,13},{6,14},{7,15},{8,0},{9,1},{1... | collective-permute-start | bytes 442376 | tf_op jit(solution)/shard_map/ppermute | solution.py:509
  47.7 4.2 %collective-permute-start.12 = (bf16[4,2,16,128]{3,2,1,0:T(8,128)(2,1)S(1)}, bf16[4,2,16,128]{3,2,1,0:T(8,128)(2,1)S(1)}, u32[]{:S(2)}, u32[]{:S(2)}) collective-permute-start(bf16[4,2,16,128]{3,2,1,0:T(8,128)(2,1)S(1)} %bitcast.4), channel_id=1, source_target_pairs={{0,5},{1,4},{2,7},{3,6},{4,13},{5,12},{6,15},{7,14},{8,1},{9,0},{1... | collective-permute-start | bytes 98312 | tf_op jit(solution)/shard_map/ppermute | solution.py:509
  52.0 0.6 copy-start.9
  52.0 0.7 copy-start.7
  52.0 0.7 copy-start.8
  52.0 0.8 copy-start.6
